TPU v7x, 512 devices: a whole 4x8x8 slice. The times are simulated.
512 devices in a mesh: row: 64 (over x, y, core), col: 8 (over z).
Axes of the slice: x: 4, y: 8, z: 8, core: 2. Of those that a mesh axis runs over, the one named last changes fastest.
Arguments:
- pivot: float32 [1024, 1024], P('row')
- panel: bfloat16 [65536, 1024], P('row', 'col'), may hold values from -6 to 6
- slab: bfloat16 [65536, 2048], P('row', 'col'), may hold values from -6 to 6
- pattern: int32 [512, 16], P('row', 'col'), may hold values 0 or 1
- col_source: int32 [16], P('col'), may hold values from 0 to 511, as said below
Outputs:
- factor_panel: bfloat16 [65536, 1024], P('row', 'col')
- updated_slab: bfloat16 [65536, 2048], P('row', 'col')
Inputs may be any that keep to these rules, and one draw needn't show every extreme that they name: `col_source`: distinct block rows; block rows 0 and 511 are always among them.
All inputs are finite; a program needn't handle non-finite values. No bound on the sum of `pattern` on one device may be relied on, other than what follows from the above.
Results may differ from a plain program's by a relative error of at most 0.015.
Values may be sent and summed in bfloat16 or wider, within the bound.
A program may use at most 64 MiB of HBM per device.

v0:
```python
import jax
import jax.numpy as jnp
from jax import lax
from jax.sharding import PartitionSpec as P

BLOCK = 128


def from_root(value, axis, source):
    kept = jnp.where(lax.axis_index(axis) == source, value, 0).astype(value.dtype)
    return lax.psum(kept, axis)


def shards(pivot, panel, slab, pattern, col_source):
    shard_width = panel.shape[1]
    full_pivot = lax.all_gather(pivot.astype(jnp.bfloat16), "row", axis=0, tiled=True).astype(
        pivot.dtype
    )
    pivot_factor = jnp.linalg.cholesky(full_pivot)
    rows_full = lax.all_gather(panel, "col", axis=1, tiled=True)
    col_index = lax.axis_index("col")
    solved = jax.scipy.linalg.solve_triangular(
        pivot_factor, rows_full.astype(jnp.float32).T, lower=True
    ).T
    factor_rows = solved.astype(jnp.bfloat16)
    own_part = lax.dynamic_slice_in_dim(factor_rows, col_index * shard_width, shard_width, 1)
    row_blocks = slab.shape[0] // BLOCK
    col_blocks = slab.shape[1] // BLOCK
    fetched = []
    for column in range(col_blocks):
        target = col_source[column]
        owner_row = target // row_blocks
        local_slot = target % row_blocks
        fragment = lax.dynamic_slice_in_dim(factor_rows, local_slot * BLOCK, BLOCK, 0)
        fetched.append(from_root(fragment, "row", owner_row))
    picked = jnp.concatenate(fetched, axis=0)
    update = jnp.dot(factor_rows, picked.T, preferred_element_type=jnp.float32)
    widened = jnp.repeat(jnp.repeat(pattern.astype(jnp.float32), BLOCK, axis=0), BLOCK, axis=1)
    updated_slab = (widened * (slab.astype(jnp.float32) - update)).astype(jnp.bfloat16)
    return (own_part, updated_slab)


def solution(mesh):
    return jax.shard_map(
        shards,
        mesh=mesh,
        in_specs=(P("row", None), P("row", "col"), P("row", "col"), P("row", "col"), P("col")),
        out_specs=(P("row", "col"), P("row", "col")),
        check_vma=False,
    )
```

profile of v0, /device:TPU:1, one launch (start us, length us, event | category | flops | bytes accessed | tf_op | source)
XLA Modules:
  0.0 712.6 jit_solution(11041099078526468622)
XLA Ops:
  15.9 46.6 %all-gather.5.cloned.1.call-done = bf16[1024,1024]{1,0:T(8,128)(2,1)} async-done(((bf16[1024,128]{1,0:T(8,128)(2,1)}), bf16[1024,1024]{1,0:T(8,128)(2,1)}) %all-gather.5.cloned.1.call-update) | async-done | bytes 2097168 | tf_op jit(solution)/shard_map/all_gather | solution.py:20
  66.4 85.3 %all-gather.3.cloned.1.call-done = bf16[1024,1024]{1,0:T(8,128)(2,1)} async-done(((bf16[16,1024]{1,0:T(8,128)(2,1)}), bf16[1024,1024]{1,0:T(8,128)(2,1)}) %all-gather.3.cloned.1.call-update) | async-done | bytes 2097168 | tf_op jit(solution)/shard_map/all_gather | solution.py:16
  162.5 11.7 %cholesky.223 = f32[128,128]{1,0:T(8,128)S(1)} custom-call(f32[128,128]{1,0:T(8,128)S(1)} %cholesky.580), custom_call_target="Cholesky" | custom-call | tf_op jit(solution)/shard_map/jit(cholesky)/cholesky | solution.py:19
  174.3 9.8 %custom-call.63 = f32[1,128,128]{1,2,0:T(8,128)S(1)} custom-call(f32[1,128,128]{2,1,0:T(8,128)S(1)} %get-tuple-element.66), custom_call_target="InvertDiagBlocksLowerTriangular" | custom-call | tf_op jit(solution)/shard_map/jit(cholesky)/cholesky | solution.py:19
  190.5 11.7 %cholesky.244 = f32[128,128]{1,0:T(8,128)S(1)} custom-call(f32[128,128]{1,0:T(8,128)S(1)} %cholesky.584), custom_call_target="Cholesky" | custom-call | tf_op jit(solution)/shard_map/jit(cholesky)/cholesky | solution.py:19
  202.9 10.1 %custom-call.64 = f32[1,128,128]{1,2,0:T(8,128)S(1)} custom-call(f32[1,128,128]{2,1,0:T(8,128)S(1)} %get-tuple-element.63), custom_call_target="InvertDiagBlocksLowerTriangular" | custom-call | tf_op jit(solution)/shard_map/jit(cholesky)/cholesky | solution.py:19
  216.3 11.7 %cholesky.468 = f32[128,128]{1,0:T(8,128)S(1)} custom-call(f32[128,128]{1,0:T(8,128)S(1)} %cholesky.589), custom_call_target="Cholesky" | custom-call | tf_op jit(solution)/shard_map/jit(cholesky)/cholesky | solution.py:19
  229.4 9.8 %custom-call.65 = f32[1,128,128]{1,2,0:T(8,128)S(1)} custom-call(f32[1,128,128]{2,1,0:T(8,128)S(1)} %get-tuple-element.60), custom_call_target="InvertDiagBlocksLowerTriangular" | custom-call | tf_op jit(solution)/shard_map/jit(cholesky)/cholesky | solution.py:19
  242.7 11.9 %cholesky.487 = f32[128,128]{1,0:T(8,128)S(1)} custom-call(f32[128,128]{1,0:T(8,128)S(1)} %cholesky.594), custom_call_target="Cholesky" | custom-call | tf_op jit(solution)/shard_map/jit(cholesky)/cholesky | solution.py:19
  256.0 9.8 %custom-call.66 = f32[1,128,128]{1,2,0:T(8,128)S(1)} custom-call(f32[1,128,128]{2,1,0:T(8,128)S(1)} %get-tuple-element.57), custom_call_target="InvertDiagBlocksLowerTriangular" | custom-call | tf_op jit(solution)/shard_map/jit(cholesky)/cholesky | solution.py:19
  269.3 11.7 %cholesky.506 = f32[128,128]{1,0:T(8,128)S(1)} custom-call(f32[128,128]{1,0:T(8,128)S(1)} %cholesky.599), custom_call_target="Cholesky" | custom-call | tf_op jit(solution)/shard_map/jit(cholesky)/cholesky | solution.py:19
  282.3 9.8 %custom-call.67 = f32[1,128,128]{1,2,0:T(8,128)S(1)} custom-call(f32[1,128,128]{2,1,0:T(8,128)S(1)} %get-tuple-element.54), custom_call_target="InvertDiagBlocksLowerTriangular" | custom-call | tf_op jit(solution)/shard_map/jit(cholesky)/cholesky | solution.py:19
  295.6 11.7 %cholesky.526 = f32[128,128]{1,0:T(8,128)S(1)} custom-call(f32[128,128]{1,0:T(8,128)S(1)} %cholesky.604), custom_call_target="Cholesky" | custom-call | tf_op jit(solution)/shard_map/jit(cholesky)/cholesky | solution.py:19
  308.7 9.8 %custom-call.68 = f32[1,128,128]{1,2,0:T(8,128)S(1)} custom-call(f32[1,128,128]{2,1,0:T(8,128)S(1)} %get-tuple-element.51), custom_call_target="InvertDiagBlocksLowerTriangular" | custom-call | tf_op jit(solution)/shard_map/jit(cholesky)/cholesky | solution.py:19
  321.5 11.7 %cholesky.546 = f32[128,128]{1,0:T(8,128)S(1)} custom-call(f32[128,128]{1,0:T(8,128)S(1)} %cholesky.609), custom_call_target="Cholesky" | custom-call | tf_op jit(solution)/shard_map/jit(cholesky)/cholesky | solution.py:19
  334.6 10.2 %custom-call.69 = f32[1,128,128]{1,2,0:T(8,128)S(1)} custom-call(f32[1,128,128]{2,1,0:T(8,128)S(1)} %get-tuple-element.48), custom_call_target="InvertDiagBlocksLowerTriangular" | custom-call | tf_op jit(solution)/shard_map/jit(cholesky)/cholesky | solution.py:19
  347.4 11.7 %cholesky.564 = f32[128,128]{1,0:T(8,128)S(1)} custom-call(f32[128,128]{1,0:T(8,128)S(1)} %convolution_subtract_fusion.12), custom_call_target="Cholesky" | custom-call | tf_op jit(solution)/shard_map/jit(cholesky)/cholesky | solution.py:19
  366.3 4.8 select_select_fusion
  371.1 22.6 %while.1 = (s32[]{:T(128)}, f32[1024,1024]{1,0:T(8,128)}, s32[8,2]{0,1:T(2,128)S(1)}, f32[8,128,128]{2,1,0:T(8,128)S(1)}, s32[]{:T(128)}) while((s32[]{:T(128)}, f32[1024,1024]{1,0:T(8,128)}, s32[8,2]{0,1:T(2,128)S(1)}, f32[8,128,128]{2,1,0:T(8,128)S(1)}, s32[]{:T(128)}) %tuple.61), condition=%wide.while_cond, body=%wide.while_body.sunk | while | flops 2 | bytes 131181 | solution.py:22
  393.7 78.8 %custom-call.70 = f32[8,128,128]{1,2,0:T(8,128)S(1)} custom-call(f32[8,128,128]{2,1,0:T(8,128)S(1)} %get-tuple-element.9), custom_call_target="InvertDiagBlocksLowerTriangular" | custom-call | tf_op jit(solution)/shard_map/jit(_solve_triangular)/triangular_solve | solution.py:22
  490.6 5.6 convolution_subtract_fusion.3
  497.0 6.1 convolution_subtract_fusion.2
  503.9 7.4 %convolution_subtract_fusion.4 = f32[128,1024]{0,1:T(8,128)S(1)} fusion(f32[896,1024]{1,0:T(8,128)S(1)} %constant_dynamic-update-slice_fusion.11, f32[1024,1024]{0,1:T(8,128)S(1)} %copy-done, f32[1024,1024]{1,0:T(8,128)} %get-tuple-element.137), kind=kOutput, calls=%fused_computation.29 | convolution fusion | flops 1409417216 | bytes 5177344 | tf_op jit(solution)/shard_map/jit(_solve_triangular)/triangular_solve | solution.py:22
  513.9 187.8 %all-reduce.4.cloned.1.call-done = (bf16[128,1024]{0,1:T(8,128)(2,1)}, bf16[128,1024]{0,1:T(8,128)(2,1)}) async-done(((bf16[128,1024]{0,1:T(8,128)(2,1)}, bf16[128,1024]{0,1:T(8,128)(2,1)}), (bf16[128,1024]{0,1:T(8,128)(2,1)}, bf16[128,1024]{0,1:T(8,128)(2,1)})) %all-reduce.4.cloned.1.call-update) | async-done | bytes 524304 | tf_op jit(solution)/shard_map/psum | solution.py:11
  (111 shorter events, 102.0 us)
Async XLA Ops:
  7.2 55.3 %all-gather.5.cloned.1.call-start = ((), (), s32[]{:S(2)}) async-start(), calls=%async_computation.1 | async-start | bytes 2359296 | tf_op jit(solution)/shard_map/all_gather | solution.py:20
  7.9 143.8 %all-gather.3.cloned.1.call-start = ((), (), s32[]{:S(2)}) async-start(), calls=%async_computation | async-start | bytes 2129920 | tf_op jit(solution)/shard_map/all_gather | solution.py:16
  9.4 692.3 %all-reduce.4.cloned.1.call-start = ((), (), s32[]{:S(2)}) async-start(), calls=%async_computation.2 | async-start | bytes 1048576 | tf_op jit(solution)/shard_map/psum | solution.py:11
  160.5 2.0 copy-start.1
  472.5 4.5 copy-start
  503.9 9.0 %copy-start.2 = (s32[8,2]{0,1:T(2,128)S(1)}, s32[8,2]{0,1:T(2,128)}, u32[]{:S(2)}) copy-start(s32[8,2]{0,1:T(2,128)} %param.8) | copy-start | bytes 196
  511.3 191.7 %copy-start.3 = (bf16[1024,256]{1,0:T(8,128)(2,1)S(1)}, bf16[1024,256]{1,0:T(8,128)(2,1)}, u32[]{:S(2)}) copy-start(bf16[1024,256]{1,0:T(8,128)(2,1)} %param.7) | copy-start | bytes 1572868
Sparse Core Ops, SparseCore 0:
  10.0 52.4 all-gather.4
  66.4 85.3 all-gather.2
  513.0 188.6 all-reduce.3
where the time goes:
time: 724 us; the launch traced here: 713 us
  waiting for transfers between devices  320 us (44%)
  other arithmetic  265 us (37%)
  matrix products  64.2 us (9%)
  local copies, waits for them, and re-layouts  37.4 us (5%)
  between operations  24.9 us (3%)
    psum x1, waiting for transfers between devices, from_root(): return lax.psum(kept, axis)  188 us
    another operation x30, other arithmetic, shards(): pivot_factor = jnp.linalg.cholesky(full_pivot)  173 us
    all_gather x1, waiting for transfers between devices, shards(): lax.all_gather(pivot.astype(jnp.bfloat16), 'row', axis=0, tiled=True)  85.3 us
    another operation x3, other arithmetic, shards(): jax.scipy.linalg.solve_triangular(pivot_factor, rows_full.astype(jnp.floa...  83.6 us
    all_gather x1, waiting for transfers between devices, shards(): rows_full = lax.all_gather(panel, 'col', axis=1, tiled=True)  46.6 us
    another operation x15, matrix products, shards(): jax.scipy.linalg.solve_triangular(pivot_factor, rows_full.astype(jnp.floa...  38.2 us
    another operation x14, matrix products, shards(): pivot_factor = jnp.linalg.cholesky(full_pivot)  23.3 us
    another operation x24, local copies, waits for them, and re-layouts  22.4 us
  transfers between devices with their start and end apart: 3, of which 3 were waited for; matrix products, arithmetic and copies ran while one was open for 1% of the time, Pallas kernels for 0%

commit v1 on v0

v1 whole, which is shorter than its diff:
```python
import jax
import jax.numpy as jnp
from jax import lax
from jax.experimental import pallas as pl
from jax.experimental.pallas import tpu as pltpu
from jax.sharding import PartitionSpec as P

F32, BF16, I32 = jnp.float32, jnp.bfloat16, jnp.int32
B = 128
NB = 8
N = 1024
MESH = pl.DeviceIdType.MESH
GROUPS = ((0, 1), (1, 2), (2, 4), (4, 8))
NT = (((1,), (1,)), ((), ()))
NN = (((1,), (0,)), ((), ()))


def dot(a, b, dims=NT):
    return lax.dot_general(a, b, dims, preferred_element_type=F32)


def lane_spread(x, lane):
    return jnp.broadcast_to(x[:, lane : lane + 1], (8, B))


def row_spread(x, row):
    return jnp.broadcast_to(x[row : row + 1, :], (8, B))


def factor(rows, w_ref, aside):
    lane = lax.broadcasted_iota(I32, (8, B), 1)
    sub = lax.broadcasted_iota(I32, (8, B), 0)
    rows = list(rows)
    before = None
    for p in range(16):
        cols = [lane_spread(rows[p], 8 * p + j) for j in range(8)]
        inside = (lane >= 8 * p) & (lane < 8 * p + 8)
        unit = jnp.where(lane == 8 * p + sub, 1.0, 0.0).astype(F32)
        low = jnp.where(inside, unit, rows[p])
        full = low
        inverse = jnp.zeros((8, B), F32)
        for k in range(8):
            inv = 1.0 / row_spread(cols[k], k)
            mult = cols[k] * inv
            both = jnp.where(sub == k, 0.0, mult)
            below = jnp.where(sub > k, mult, 0.0)
            full = full - both * row_spread(full, k)
            low = low - below * row_spread(low, k)
            inverse = jnp.where(sub == k, inv, inverse)
            for j in range(k + 1, 8):
                cols[j] = cols[j] - both * row_spread(cols[j], k)
        w = jnp.where(lane < 8 * p + 8, low * jnp.sqrt(inverse), 0.0)
        if p % 2 == 0:
            before = w
        else:
            w_ref[8 * p - 8 : 8 * p + 8, :] = jnp.concatenate([before, w], 0).astype(BF16)
        full = full * inverse
        spread = [row_spread(full, k) for k in range(8)]
        for q in range(p + 1, 16):
            v = rows[q]
            t = [lane_spread(v, 8 * p + k) * spread[k] for k in range(8)]
            total = ((t[0] + t[1]) + (t[2] + t[3])) + ((t[4] + t[5]) + (t[6] + t[7]))
            rows[q] = jnp.where(inside, 0.0, v) - total
        aside(p)


def kernel(
    pivot, panel, slab, pattern, col_source, own_out, slab_out,
    piv, cs, marked, part1, part2, part3, pick, rows, lu, tcol, quad, w_ref, low_w, fac,
    y_send, y_recv, q_send, q_recv, c_send, c_recv, p_send, p_recv,
    s1_send, s1_recv, s2_send, s2_recv, s3_send, s3_recv, s4_send, s4_recv, s5_send, s5_recv,
):
    r = lax.axis_index("row")
    z = lax.axis_index("col")
    x, y, core = r // 16, (r // 2) % 8, r % 2
    q = x * 2 + core

    def at_y(d):
        return ((x * 8 + (y + d) % 8) * 2 + core, z)

    def at_q(d):
        o = (q + d) % 8
        return (((o // 2) * 8 + y) * 2 + o % 2, z)

    def at_z(d):
        return (r, (z + d) % 8)

    def remote(src, dst, send, recv, device):
        return pltpu.make_async_remote_copy(
            src_ref=src, dst_ref=dst, send_sem=send, recv_sem=recv,
            device_id=device, device_id_type=MESH,
        )

    def y_copy(g, d):
        a, b = GROUPS[g]
        ref = piv.at[a:b, x * 8 + y, core]
        return remote(ref, ref, y_send.at[g, d], y_recv.at[g, d], at_y(d))

    def q_copy(g, d):
        a, b = GROUPS[g]
        ref = piv.at[a:b, pl.ds(x * 8, 8), core]
        return remote(ref, ref, q_send.at[g, d], q_recv.at[g, d], at_q(d))

    def c_copy(d):
        ref = cs.at[z]
        return remote(ref, ref, c_send.at[d], c_recv.at[d], at_z(d))

    def p_copy(d):
        return remote(panel, rows.at[z], p_send.at[d], p_recv.at[d], at_z(d))

    def s1_copy(d):
        return remote(
            marked.at[(q + d) % 8], part1.at[d], s1_send.at[d], s1_recv.at[d], at_q(d)
        )

    def s2_copy(d):
        return remote(
            part2.at[0, pl.ds(((y + d) % 8) * 32, 32)], part2.at[d, 0:32],
            s2_send.at[d], s2_recv.at[d], at_y(d),
        )

    def s3_copy(source):
        return remote(
            part3.at[0], part3.at[1 + source], s3_send, s3_recv.at[source], (r, q)
        )

    def s4_copy(d):
        ref = pick.at[y]
        return remote(ref, ref, s4_send.at[d], s4_recv.at[d], at_q(d))

    def s5_copy(d):
        ref = pick.at[y]
        return remote(ref, ref, s5_send.at[d], s5_recv.at[d], at_y(d))

    others = range(1, 8)

    barrier = pltpu.get_barrier_semaphore()
    for d in others:
        for device in (at_y(d), at_q(d), at_z(d)):
            pl.semaphore_signal(barrier, inc=1, device_id=device, device_id_type=MESH)

    for c in range(NB):
        piv[c, x * 8 + y, core] = pivot[:, c * B : (c + 1) * B].astype(BF16)
    sub = lax.broadcasted_iota(I32, (8, B), 0)
    cs[z] = jnp.where(sub == 0, col_source[0], col_source[1])

    pl.semaphore_wait(barrier, 21)
    for d in others:
        y_copy(0, d).start()
    for d in others:
        c_copy(d).start()
    for g in (1, 2, 3):
        for d in others:
            y_copy(g, d).start()
    rows[z] = panel[...]
    lu[...] = jnp.zeros_like(lu)
    quad[...] = jnp.zeros_like(quad)
    tcol[...] = jnp.zeros_like(tcol)
    w_ref[...] = jnp.zeros_like(w_ref)
    for d in others:
        y_copy(0, d).wait_recv()
    for d in others:
        q_copy(0, d).start()

    for d in others:
        c_copy(d).wait_recv()

    def mark(pair, carry):
        for t in range(2):
            wanted = cs[pair, t : t + 1, :]
            total = jnp.zeros((B, B), F32)
            for s in range(8):
                here = panel[s * B : (s + 1) * B, :].astype(F32)
                total = jnp.where(wanted == r * 8 + s, here, total)
            marked[pair, t * B : (t + 1) * B, :] = total.astype(BF16)
        return carry

    lax.fori_loop(0, 8, mark, 0)
    for g in (1, 2):
        for d in others:
            y_copy(g, d).wait_recv()
        for d in others:
            q_copy(g, d).start()
    for d in others:
        s1_copy(d).start()
    for d in others:
        p_copy(d).start()
    for d in others:
        y_copy(3, d).wait_recv()
    for d in others:
        q_copy(3, d).start()

    def block_rows(column, block):
        return piv[column, pl.ds(block * 4, 4)].reshape(B, B)

    def arrive(j):
        for g, (a, _) in enumerate(GROUPS):
            @pl.when(j == a)
            def _():
                for d in others:
                    q_copy(g, d).wait_recv()

        @pl.when(j == 1)
        def _():
            total = marked[q].astype(F32)
            for d in others:
                s1_copy(d).wait_recv()
            for d in others:
                total += part1[d].astype(F32)
            part2[0] = total.astype(BF16)
            for d in others:
                s2_copy(d).start()

        @pl.when(j == 2)
        def _():
            for d in others:
                s2_copy(d).wait_recv()
            total = part2[0, pl.ds(y * 32, 32), :].astype(F32)
            for d in others:
                total += part2[d, 0:32, :].astype(F32)
            part3[0] = total.astype(BF16)

            @pl.when(z != q)
            def _():
                s3_copy(z).start()

        @pl.when((j == 3) & (z == q))
        def _():
            for s in range(8):
                @pl.when(z != s)
                def _():
                    s3_copy(s).wait_recv()
                    pick[y, s] = part3[1 + s]
            pick[y, z] = part3[0]
            for d in others:
                s4_copy(d).start()

        @pl.when(j == 4)
        def _():
            for d in others:
                @pl.when((q + 8 - d) % 8 == z)
                def _():
                    s4_copy(d).wait_recv()
            for d in others:
                s5_copy(d).start()

    def step(j, carry):
        arrive(j)
        jm = jnp.maximum(j - 1, 0)
        jn = jnp.minimum(j + 1, NB - 1)
        now = pl.ds(pl.multiple_of(j * B, B), B)
        last = pl.ds(pl.multiple_of(jm * B, B), B)
        after = pl.ds(pl.multiple_of(jn * B, B), B)
        w_old = w_ref[...]
        row_j = lu[0, now, :]
        diagonal = block_rows(j, j).astype(F32) - quad[...]
        eye = jnp.where(
            lax.broadcasted_iota(I32, (B, B), 0) == lax.broadcasted_iota(I32, (B, B), 1), 1.0, 0.0
        ).astype(F32)

        def aside(p):
            block, half = p // 2, p % 2
            part = slice(p * 64, (p + 1) * 64)
            was_below = jnp.where(block > jm, 0, 1)
            done = dot(tcol[part, :], w_old).astype(BF16)
            lu[was_below, part, last] = done
            upper = jnp.where(block > j, 0, 1)
            t = -dot(lu[upper, part, :], row_j)
            source = piv[j, block * 4 + half * 2 : block * 4 + half * 2 + 2].reshape(64, B)
            keep = jnp.where(block > j, 1.0, 0.0).astype(F32)
            on = jnp.where(block == j, 1.0, 0.0).astype(F32)
            t = t + source.astype(F32) * keep + eye[half * 64 : half * 64 + 64, :] * on
            tcol[part, :] = t.astype(BF16)

        factor([diagonal[8 * i : 8 * i + 8, :] for i in range(16)], w_ref, aside)
        row_next = lu[0, after, :]
        total = dot(row_next, row_next)
        new = dot(tcol[after, :], w_ref[...]).astype(BF16)
        quad[...] = total + dot(new, new)
        lu[0, after, now] = new
        return carry

    lax.fori_loop(0, NB, step, 0)
    for i in range(4):
        part = slice(i * 256, (i + 1) * 256)
        lu[1, part, N - B : N] = dot(tcol[part, :], w_ref[...]).astype(BF16)

    for d in others:
        s5_copy(d).wait_recv()
    raw = jnp.concatenate(
        [jnp.concatenate([pick[i, c] for i in range(8)], axis=0) for c in range(NB)], axis=1
    )
    for c in range(4):
        cols = slice(c * 256, (c + 1) * 256)
        deep = (c + 1) * 256
        low_w[:, cols] = dot(raw[:, :deep], lu[1, :deep, cols], NN).astype(BF16)
    for d in others:
        p_copy(d).wait_recv()
    for i in range(8):
        part = slice(i * B, (i + 1) * B)
        mine = jnp.concatenate([rows[c, part, :] for c in range(NB)], axis=1)
        for c in range(4):
            cols = slice(c * 256, (c + 1) * 256)
            deep = (c + 1) * 256
            fac[part, cols] = dot(mine[:, :deep], lu[1, :deep, cols], NN).astype(BF16)
        own_out[part, :] = fac[part, pl.ds(pl.multiple_of(z * B, B), B)]
        update = dot(fac[part, :], low_w[...])
        left = slab[part, :].astype(F32) - update
        for c in range(2):
            cols = slice(c * B, (c + 1) * B)
            slab_out[part, cols] = (left[:, cols] * pattern[i, c].astype(F32)).astype(BF16)

    for d in others:
        for g in range(4):
            y_copy(g, d).wait_send()
            q_copy(g, d).wait_send()
        c_copy(d).wait_send()
        p_copy(d).wait_send()
        s1_copy(d).wait_send()
        s2_copy(d).wait_send()
        s5_copy(d).wait_send()

        @pl.when(z == q)
        def _():
            s4_copy(d).wait_send()

    @pl.when(z != q)
    def _():
        s3_copy(z).wait_send()


def shards(pivot, panel, slab, pattern, col_source):
    vmem = pl.BlockSpec(memory_space=pltpu.VMEM)
    smem = pl.BlockSpec(memory_space=pltpu.SMEM)
    dma = pltpu.SemaphoreType.DMA
    return pl.pallas_call(
        kernel,
        out_shape=[
            jax.ShapeDtypeStruct((N, B), BF16),
            jax.ShapeDtypeStruct((N, 2 * B), BF16),
        ],
        in_specs=[vmem, vmem, vmem, smem, smem],
        out_specs=[vmem, vmem],
        scratch_shapes=[
            pltpu.VMEM((8, 32, 2, 16, B), BF16),
            pltpu.VMEM((8, 8, B), I32),
            pltpu.VMEM((8, 2 * B, B), BF16),
            pltpu.VMEM((8, 2 * B, B), BF16),
            pltpu.VMEM((8, 2 * B, B), BF16),
            pltpu.VMEM((9, 32, B), BF16),
            pltpu.VMEM((8, 8, 32, B), BF16),
            pltpu.VMEM((8, N, B), BF16),
            pltpu.VMEM((2, N, N), BF16),
            pltpu.VMEM((N, B), BF16),
            pltpu.VMEM((B, B), F32),
            pltpu.VMEM((B, B), BF16),
            pltpu.VMEM((2 * B, N), BF16),
            pltpu.VMEM((N, N), BF16),
            dma((4, 8)), dma((4, 8)), dma((4, 8)), dma((4, 8)),
            dma((8,)), dma((8,)), dma((8,)), dma((8,)),
            dma((8,)), dma((8,)), dma((8,)), dma((8,)),
            dma, dma((8,)),
            dma((8,)), dma((8,)), dma((8,)), dma((8,)),
        ],
        compiler_params=pltpu.CompilerParams(
            collective_id=0, has_side_effects=True, vmem_limit_bytes=56 * 2**20
        ),
        cost_estimate=pl.CostEstimate(
            flops=5 * 10**9, bytes_accessed=2 * 2**20, transcendentals=0
        ),
    )(pivot, panel, slab, pattern, col_source)


def solution(mesh):
    return jax.shard_map(
        shards,
        mesh=mesh,
        in_specs=(P("row", None), P("row", "col"), P("row", "col"), P("row", "col"), P("col")),
        out_specs=(P("row", "col"), P("row", "col")),
        check_vma=False,
    )
```

time: 724 us -> 108 us (0.15)
  the two profiles are of different devices: /device:TPU:1 before, /device:TPU:5 now
where the time goes in v1:
time: 108 us; the launch traced here: 107 us
  Pallas kernels  103 us (95%)
  local copies, waits for them, and re-layouts  3.87 us (4%)
    pallas_call x1, Pallas kernels, shards(): pl.pallas_call(kernel, out_shape=[jax.ShapeDtypeStruct((N, B), BF16), jax...  103 us
    unnamed x5, local copies, waits for them, and re-layouts  3.87 us

profile of v1, /device:TPU:5, one launch (start us, length us, event | category | flops | bytes accessed | tf_op | source)
XLA Modules:
  0.0 107.3 jit_solution(4512201571199385356)
XLA Ops:
  0.6 1.3 %copy.7.pattern = s32[8,2]{1,0:T(8,128)} copy(s32[8,2]{0,1:T(2,128)} %param.8) | data formatting | bytes 128 | tf_op args[3]
  2.0 102.8 %shard_map.68 = (bf16[1024,128]{1,0:T(8,128)(2,1)}, bf16[1024,256]{1,0:T(8,128)(2,1)}) custom-call(f32[16,1024]{1,0:T(8,128)} %pivot.1, bf16[1024,128]{1,0:T(8,128)(2,1)} %panel.1, bf16[1024,256]{1,0:T(8,128)(2,1)} %slab.1, s32[8,2]{1,0:T(8,128)} %copy.7.pattern, s32[2]{0:T(128)} %col_source.1), custom_call_target="tpu_custom_call" | custom-call | flops 5000000000 | bytes 2097152 | tf_op jit(solution)/shard_map/pallas_call | solution.py:336
  104.8 0.0 copy-start
  104.8 1.7 %copy.10 = bf16[1024,128]{1,0:T(8,128)(2,1)} copy(bf16[1024,128]{1,0:T(8,128)(2,1)} %get-tuple-element.4) | data formatting | bytes 524288
  106.5 0.0 copy-done
  106.5 0.8 copy.11
Async XLA Ops:
  104.8 1.7 %copy-start = (bf16[1024,256]{1,0:T(8,128)(2,1)S(1)}, bf16[1024,256]{1,0:T(8,128)(2,1)}, u32[]{:S(2)}) copy-start(bf16[1024,256]{1,0:T(8,128)(2,1)} %get-tuple-element.5) | copy-start | bytes 1572868

commit v2 on v1

--- a/solution.py
+++ b/solution.py
@@ -10,7 +10,6 @@
 NB = 8
 N = 1024
 MESH = pl.DeviceIdType.MESH
-GROUPS = ((0, 1), (1, 2), (2, 4), (4, 8))
 NT = (((1,), (1,)), ((), ()))
 NN = (((1,), (0,)), ((), ()))
 
@@ -32,8 +31,12 @@
     sub = lax.broadcasted_iota(I32, (8, B), 0)
     rows = list(rows)
     before = None
+    cols = [lane_spread(rows[0], j) for j in range(8)]
     for p in range(16):
-        cols = [lane_spread(rows[p], 8 * p + j) for j in range(8)]
+        more = p < 15
+        if more:
+            left = [lane_spread(rows[p + 1], 8 * p + j) for j in range(8)]
+            ahead = [lane_spread(rows[p + 1], 8 * p + 8 + j) for j in range(8)]
         inside = (lane >= 8 * p) & (lane < 8 * p + 8)
         unit = jnp.where(lane == 8 * p + sub, 1.0, 0.0).astype(F32)
         low = jnp.where(inside, unit, rows[p])
@@ -44,11 +47,19 @@
             mult = cols[k] * inv
             both = jnp.where(sub == k, 0.0, mult)
             below = jnp.where(sub > k, mult, 0.0)
+            across = [None] * 8
+            for j in range(k + 1, 8):
+                across[j] = row_spread(cols[j], k)
+                cols[j] = cols[j] - both * across[j]
+            if more:
+                mult = left[k] * inv
+                for j in range(8):
+                    ahead[j] = ahead[j] - mult * row_spread(left[k], j)
+                for j in range(k + 1, 8):
+                    left[j] = left[j] - mult * across[j]
             full = full - both * row_spread(full, k)
             low = low - below * row_spread(low, k)
             inverse = jnp.where(sub == k, inv, inverse)
-            for j in range(k + 1, 8):
-                cols[j] = cols[j] - both * row_spread(cols[j], k)
         w = jnp.where(lane < 8 * p + 8, low * jnp.sqrt(inverse), 0.0)
         if p % 2 == 0:
             before = w
@@ -61,13 +72,15 @@
             t = [lane_spread(v, 8 * p + k) * spread[k] for k in range(8)]
             total = ((t[0] + t[1]) + (t[2] + t[3])) + ((t[4] + t[5]) + (t[6] + t[7]))
             rows[q] = jnp.where(inside, 0.0, v) - total
+        if more:
+            cols = ahead
         aside(p)
 
 
 def kernel(
     pivot, panel, slab, pattern, col_source, own_out, slab_out,
     piv, cs, marked, part1, part2, part3, pick, rows, lu, tcol, quad, w_ref, low_w, fac,
-    y_send, y_recv, q_send, q_recv, c_send, c_recv, p_send, p_recv,
+    y_send, y_recv, q_send, q_recv, x_send, x_recv, k_send, k_recv, c_send, c_recv, p_send, p_recv,
     s1_send, s1_recv, s2_send, s2_recv, s3_send, s3_recv, s4_send, s4_recv, s5_send, s5_recv,
 ):
     r = lax.axis_index("row")
@@ -82,6 +95,9 @@
         o = (q + d) % 8
         return (((o // 2) * 8 + y) * 2 + o % 2, z)
 
+    def at_x(d):
+        return ((((x + d) % 4) * 8 + y) * 2 + core, z)
+
     def at_z(d):
         return (r, (z + d) % 8)
 
@@ -92,21 +108,44 @@
         )
 
     def y_copy(g, d):
-        a, b = GROUPS[g]
-        ref = piv.at[a:b, x * 8 + y, core]
+        ref = piv.at[0:1, x * 8 + y, core] if g == 0 else piv.at[1:8, x * 8 + y, core]
         return remote(ref, ref, y_send.at[g, d], y_recv.at[g, d], at_y(d))
 
     def q_copy(g, d):
-        a, b = GROUPS[g]
-        ref = piv.at[a:b, pl.ds(x * 8, 8), core]
+        ref = piv.at[g : g + 1, pl.ds(x * 8, 8), core]
         return remote(ref, ref, q_send.at[g, d], q_recv.at[g, d], at_q(d))
+
+    def x_copy(g, d):
+        ref = piv.at[2 * g : 4 * g, pl.ds(x * 8, 8), core]
+        return remote(ref, ref, x_send.at[g, d], x_recv.at[g, d], at_x(d))
+
+    def k_copy(g):
+        ref = piv.at[2 * g : 4 * g, :, core]
+        return remote(ref, ref, k_send.at[g], k_recv.at[g], (r + 1 - 2 * core, z))
 
     def c_copy(d):
         ref = cs.at[z]
         return remote(ref, ref, c_send.at[d], c_recv.at[d], at_z(d))
 
-    def p_copy(d):
-        return remote(panel, rows.at[z], p_send.at[d], p_recv.at[d], at_z(d))
+    def p_copy(hop, way):
+        if way == 0:
+            block, device = (z + 8 - hop) % 8, (r, (z + 1) % 8)
+        else:
+            block, device = (z + hop) % 8, (r, (z + 7) % 8)
+        if hop == 0:
+            src, dst = panel, rows.at[z]
+        elif hop < 3:
+            src = dst = rows.at[block]
+        else:
+            src = dst = rows.at[block, way * (N // 2) : (way + 1) * (N // 2)]
+        return remote(src, dst, p_send.at[hop, way], p_recv.at[hop, way], device)
+
+    def p_hop(hop):
+        for way in range(2):
+            if hop:
+                p_copy(hop - 1, way).wait_recv()
+        for way in range(2):
+            p_copy(hop, way).start()
 
     def s1_copy(d):
         return remote(
@@ -149,9 +188,9 @@
         y_copy(0, d).start()
     for d in others:
         c_copy(d).start()
-    for g in (1, 2, 3):
-        for d in others:
-            y_copy(g, d).start()
+    for d in others:
+        y_copy(1, d).start()
+    p_hop(0)
     rows[z] = panel[...]
     lu[...] = jnp.zeros_like(lu)
     quad[...] = jnp.zeros_like(quad)
@@ -176,29 +215,51 @@
         return carry
 
     lax.fori_loop(0, 8, mark, 0)
+    for d in others:
+        y_copy(1, d).wait_recv()
+    for d in others:
+        q_copy(1, d).start()
+    for d in others:
+        s1_copy(d).start()
     for g in (1, 2):
-        for d in others:
-            y_copy(g, d).wait_recv()
-        for d in others:
-            q_copy(g, d).start()
-    for d in others:
-        s1_copy(d).start()
-    for d in others:
-        p_copy(d).start()
-    for d in others:
-        y_copy(3, d).wait_recv()
-    for d in others:
-        q_copy(3, d).start()
+        for d in range(1, 4):
+            x_copy(g, d).start()
 
     def block_rows(column, block):
         return piv[column, pl.ds(block * 4, 4)].reshape(B, B)
 
     def arrive(j):
-        for g, (a, _) in enumerate(GROUPS):
-            @pl.when(j == a)
+        for g in range(2):
+            @pl.when(j == g)
             def _():
                 for d in others:
                     q_copy(g, d).wait_recv()
+
+        @pl.when(j == 1)
+        def _():
+            p_hop(1)
+            for d in range(1, 4):
+                x_copy(1, d).wait_recv()
+            k_copy(1).start()
+
+        @pl.when(j == 2)
+        def _():
+            k_copy(1).wait_recv()
+
+        @pl.when(j == 3)
+        def _():
+            p_hop(2)
+            for d in range(1, 4):
+                x_copy(2, d).wait_recv()
+            k_copy(2).start()
+
+        @pl.when(j == 4)
+        def _():
+            k_copy(2).wait_recv()
+
+        @pl.when(j == 5)
+        def _():
+            p_hop(3)
 
         @pl.when(j == 1)
         def _():
@@ -254,6 +315,7 @@
         w_old = w_ref[...]
         row_j = lu[0, now, :]
         diagonal = block_rows(j, j).astype(F32) - quad[...]
+        lu[0, after, last] = dot(tcol[after, :], w_old).astype(BF16)
         eye = jnp.where(
             lax.broadcasted_iota(I32, (B, B), 0) == lax.broadcasted_iota(I32, (B, B), 1), 1.0, 0.0
         ).astype(F32)
@@ -267,16 +329,16 @@
             upper = jnp.where(block > j, 0, 1)
             t = -dot(lu[upper, part, :], row_j)
             source = piv[j, block * 4 + half * 2 : block * 4 + half * 2 + 2].reshape(64, B)
-            keep = jnp.where(block > j, 1.0, 0.0).astype(F32)
             on = jnp.where(block == j, 1.0, 0.0).astype(F32)
-            t = t + source.astype(F32) * keep + eye[half * 64 : half * 64 + 64, :] * on
+            t = t + jnp.where(block > j, source.astype(F32), 0.0) + eye[half * 64 : half * 64 + 64, :] * on
             tcol[part, :] = t.astype(BF16)
+            if p == 3:
+                row_next = lu[0, after, :]
+                quad[...] = dot(row_next, row_next)
 
         factor([diagonal[8 * i : 8 * i + 8, :] for i in range(16)], w_ref, aside)
-        row_next = lu[0, after, :]
-        total = dot(row_next, row_next)
         new = dot(tcol[after, :], w_ref[...]).astype(BF16)
-        quad[...] = total + dot(new, new)
+        quad[...] += dot(new, new)
         lu[0, after, now] = new
         return carry
 
@@ -294,8 +356,8 @@
         cols = slice(c * 256, (c + 1) * 256)
         deep = (c + 1) * 256
         low_w[:, cols] = dot(raw[:, :deep], lu[1, :deep, cols], NN).astype(BF16)
-    for d in others:
-        p_copy(d).wait_recv()
+    for way in range(2):
+        p_copy(3, way).wait_recv()
     for i in range(8):
         part = slice(i * B, (i + 1) * B)
         mine = jnp.concatenate([rows[c, part, :] for c in range(NB)], axis=1)
@@ -310,12 +372,18 @@
             cols = slice(c * B, (c + 1) * B)
             slab_out[part, cols] = (left[:, cols] * pattern[i, c].astype(F32)).astype(BF16)
 
-    for d in others:
-        for g in range(4):
+    for g in range(1, 3):
+        for d in range(1, 4):
+            x_copy(g, d).wait_send()
+        k_copy(g).wait_send()
+    for hop in range(4):
+        for way in range(2):
+            p_copy(hop, way).wait_send()
+    for d in others:
+        for g in range(2):
             y_copy(g, d).wait_send()
             q_copy(g, d).wait_send()
         c_copy(d).wait_send()
-        p_copy(d).wait_send()
         s1_copy(d).wait_send()
         s2_copy(d).wait_send()
         s5_copy(d).wait_send()
@@ -356,8 +424,9 @@
             pltpu.VMEM((B, B), BF16),
             pltpu.VMEM((2 * B, N), BF16),
             pltpu.VMEM((N, N), BF16),
-            dma((4, 8)), dma((4, 8)), dma((4, 8)), dma((4, 8)),
-            dma((8,)), dma((8,)), dma((8,)), dma((8,)),
+            dma((2, 8)), dma((2, 8)), dma((2, 8)), dma((2, 8)),
+            dma((3, 4)), dma((3, 4)), dma((3,)), dma((3,)),
+            dma((8,)), dma((8,)), dma((4, 2)), dma((4, 2)),
             dma((8,)), dma((8,)), dma((8,)), dma((8,)),
             dma, dma((8,)),
             dma((8,)), dma((8,)), dma((8,)), dma((8,)),

time: 108 us -> 80.5 us (0.75)
  Pallas kernels: 103 us -> 75.8 us
    pallas_call x1, Pallas kernels: 103 us -> 75.8 us  [shards(): pl.pallas_call(kernel, out_shape=[jax.ShapeDtypeStruct((N, B), BF16), jax...]
where the time goes in v2:
time: 80.5 us; the launch traced here: 80.3 us
  Pallas kernels  75.8 us (94%)
  local copies, waits for them, and re-layouts  3.87 us (5%)
    pallas_call x1, Pallas kernels, shards(): pl.pallas_call(kernel, out_shape=[jax.ShapeDtypeStruct((N, B), BF16), jax...  75.8 us
    unnamed x5, local copies, waits for them, and re-layouts  3.87 us

profile of v2, /device:TPU:5, one launch (start us, length us, event | category | flops | bytes accessed | tf_op | source)
XLA Modules:
  0.0 80.3 jit_solution(795870675660968714)
XLA Ops:
  0.6 1.3 %copy.7.pattern = s32[8,2]{1,0:T(8,128)} copy(s32[8,2]{0,1:T(2,128)} %param.8) | data formatting | bytes 128 | tf_op args[3]
  2.0 75.8 %shard_map.68 = (bf16[1024,128]{1,0:T(8,128)(2,1)}, bf16[1024,256]{1,0:T(8,128)(2,1)}) custom-call(f32[16,1024]{1,0:T(8,128)} %pivot.1, bf16[1024,128]{1,0:T(8,128)(2,1)} %panel.1, bf16[1024,256]{1,0:T(8,128)(2,1)} %slab.1, s32[8,2]{1,0:T(8,128)} %copy.7.pattern, s32[2]{0:T(128)} %col_source.1), custom_call_target="tpu_custom_call" | custom-call | flops 5000000000 | bytes 2097152 | tf_op jit(solution)/shard_map/pallas_call | solution.py:404
  77.8 0.0 copy-start
  77.8 1.7 %copy.10 = bf16[1024,128]{1,0:T(8,128)(2,1)} copy(bf16[1024,128]{1,0:T(8,128)(2,1)} %get-tuple-element.4) | data formatting | bytes 524288
  79.5 0.0 copy-done
  79.5 0.8 copy.11
Async XLA Ops:
  77.8 1.7 %copy-start = (bf16[1024,256]{1,0:T(8,128)(2,1)S(1)}, bf16[1024,256]{1,0:T(8,128)(2,1)}, u32[]{:S(2)}) copy-start(bf16[1024,256]{1,0:T(8,128)(2,1)} %get-tuple-element.5) | copy-start | bytes 1572868

commit v3 on v2

--- a/solution.py
+++ b/solution.py
@@ -10,6 +10,7 @@
 NB = 8
 N = 1024
 MESH = pl.DeviceIdType.MESH
+GROUPS = (slice(0, 1), slice(1, 2), slice(2, 4), slice(4, 8))
 NT = (((1,), (1,)), ((), ()))
 NN = (((1,), (0,)), ((), ()))
 
@@ -79,9 +80,9 @@
 
 def kernel(
     pivot, panel, slab, pattern, col_source, own_out, slab_out,
-    piv, cs, marked, part1, part2, part3, pick, rows, lu, tcol, quad, w_ref, low_w, fac,
-    y_send, y_recv, q_send, q_recv, x_send, x_recv, k_send, k_recv, c_send, c_recv, p_send, p_recv,
-    s1_send, s1_recv, s2_send, s2_recv, s3_send, s3_recv, s4_send, s4_recv, s5_send, s5_recv,
+    piv, cs, marked, part1, part2, part3, held, pick, rows, lu, tcol, quad, w_ref, low_w, fac,
+    y_send, y_recv, x_send, x_recv, k_send, k_recv, c_send, c_recv, p_send, p_recv,
+    s1_send, s1_recv, s2_send, s2_recv, s3_send, s3_recv, s4_send, s4_recv, s5_send, s5_recv, s6_send, s6_recv,
 ):
     r = lax.axis_index("row")
     z = lax.axis_index("col")
@@ -108,19 +109,15 @@
         )
 
     def y_copy(g, d):
-        ref = piv.at[0:1, x * 8 + y, core] if g == 0 else piv.at[1:8, x * 8 + y, core]
+        ref = piv.at[GROUPS[g], :, y, core] if g == 2 else piv.at[GROUPS[g], x, y, core]
         return remote(ref, ref, y_send.at[g, d], y_recv.at[g, d], at_y(d))
 
-    def q_copy(g, d):
-        ref = piv.at[g : g + 1, pl.ds(x * 8, 8), core]
-        return remote(ref, ref, q_send.at[g, d], q_recv.at[g, d], at_q(d))
-
     def x_copy(g, d):
-        ref = piv.at[2 * g : 4 * g, pl.ds(x * 8, 8), core]
+        ref = piv.at[GROUPS[g], x, y, core] if g == 2 else piv.at[GROUPS[g], x, :, core]
         return remote(ref, ref, x_send.at[g, d], x_recv.at[g, d], at_x(d))
 
     def k_copy(g):
-        ref = piv.at[2 * g : 4 * g, :, core]
+        ref = piv.at[GROUPS[g], :, :, core]
         return remote(ref, ref, k_send.at[g], k_recv.at[g], (r + 1 - 2 * core, z))
 
     def c_copy(d):
@@ -164,12 +161,19 @@
         )
 
     def s4_copy(d):
-        ref = pick.at[y]
-        return remote(ref, ref, s4_send.at[d], s4_recv.at[d], at_q(d))
+        half = (q + d) % 2
+        return remote(
+            held.at[pl.ds(half * 4, 4)], pick.at[y, pl.ds(half * 4, 4)],
+            s4_send.at[d], s4_recv.at[d], at_q(d),
+        )
 
     def s5_copy(d):
-        ref = pick.at[y]
+        ref = pick.at[y, pl.ds(core * 4, 4)]
         return remote(ref, ref, s5_send.at[d], s5_recv.at[d], at_y(d))
+
+    def s6_copy():
+        ref = pick.at[:, pl.ds(core * 4, 4)]
+        return remote(ref, ref, s6_send, s6_recv, (r + 1 - 2 * core, z))
 
     others = range(1, 8)
 
@@ -179,7 +183,7 @@
             pl.semaphore_signal(barrier, inc=1, device_id=device, device_id_type=MESH)
 
     for c in range(NB):
-        piv[c, x * 8 + y, core] = pivot[:, c * B : (c + 1) * B].astype(BF16)
+        piv[c, x, y, core] = pivot[:, c * B : (c + 1) * B].astype(BF16)
     sub = lax.broadcasted_iota(I32, (8, B), 0)
     cs[z] = jnp.where(sub == 0, col_source[0], col_source[1])
 
@@ -188,18 +192,21 @@
         y_copy(0, d).start()
     for d in others:
         c_copy(d).start()
-    for d in others:
-        y_copy(1, d).start()
-    p_hop(0)
+    for d in range(1, 4):
+        x_copy(2, d).start()
+    for g in (1, 3):
+        for d in others:
+            y_copy(g, d).start()
     rows[z] = panel[...]
     lu[...] = jnp.zeros_like(lu)
     quad[...] = jnp.zeros_like(quad)
     tcol[...] = jnp.zeros_like(tcol)
     w_ref[...] = jnp.zeros_like(w_ref)
-    for d in others:
-        y_copy(0, d).wait_recv()
-    for d in others:
-        q_copy(0, d).start()
+    for g in (0, 1):
+        for d in others:
+            y_copy(g, d).wait_recv()
+        for d in range(1, 4):
+            x_copy(g, d).start()
 
     for d in others:
         c_copy(d).wait_recv()
@@ -216,97 +223,108 @@
 
     lax.fori_loop(0, 8, mark, 0)
     for d in others:
-        y_copy(1, d).wait_recv()
-    for d in others:
-        q_copy(1, d).start()
-    for d in others:
         s1_copy(d).start()
-    for g in (1, 2):
+    for d in range(1, 4):
+        x_copy(2, d).wait_recv()
+    for d in others:
+        y_copy(2, d).start()
+    p_hop(0)
+    for g in (0, 1):
         for d in range(1, 4):
-            x_copy(g, d).start()
+            x_copy(g, d).wait_recv()
+        k_copy(g).start()
 
     def block_rows(column, block):
-        return piv[column, pl.ds(block * 4, 4)].reshape(B, B)
-
-    def arrive(j):
-        for g in range(2):
-            @pl.when(j == g)
-            def _():
-                for d in others:
-                    q_copy(g, d).wait_recv()
-
-        @pl.when(j == 1)
+        return piv[column, block // 2, pl.ds((block % 2) * 4, 4)].reshape(B, B)
+
+    def s1_on():
+        total = marked[q].astype(F32)
+        for d in others:
+            s1_copy(d).wait_recv()
+        for d in others:
+            total += part1[d].astype(F32)
+        part2[0] = total.astype(BF16)
+        for d in others:
+            s2_copy(d).start()
+
+    def s2_on():
+        for d in others:
+            s2_copy(d).wait_recv()
+        total = part2[0, pl.ds(y * 32, 32), :].astype(F32)
+        for d in others:
+            total += part2[d, 0:32, :].astype(F32)
+        part3[0] = total.astype(BF16)
+
+        @pl.when(z != q)
         def _():
-            p_hop(1)
-            for d in range(1, 4):
-                x_copy(1, d).wait_recv()
-            k_copy(1).start()
-
-        @pl.when(j == 2)
-        def _():
-            k_copy(1).wait_recv()
-
-        @pl.when(j == 3)
-        def _():
-            p_hop(2)
-            for d in range(1, 4):
-                x_copy(2, d).wait_recv()
-            k_copy(2).start()
-
-        @pl.when(j == 4)
-        def _():
-            k_copy(2).wait_recv()
-
-        @pl.when(j == 5)
-        def _():
-            p_hop(3)
-
-        @pl.when(j == 1)
-        def _():
-            total = marked[q].astype(F32)
-            for d in others:
-                s1_copy(d).wait_recv()
-            for d in others:
-                total += part1[d].astype(F32)
-            part2[0] = total.astype(BF16)
-            for d in others:
-                s2_copy(d).start()
-
-        @pl.when(j == 2)
-        def _():
-            for d in others:
-                s2_copy(d).wait_recv()
-            total = part2[0, pl.ds(y * 32, 32), :].astype(F32)
-            for d in others:
-                total += part2[d, 0:32, :].astype(F32)
-            part3[0] = total.astype(BF16)
-
-            @pl.when(z != q)
-            def _():
-                s3_copy(z).start()
-
-        @pl.when((j == 3) & (z == q))
+            s3_copy(z).start()
+
+    def s3_on():
+        @pl.when(z == q)
         def _():
             for s in range(8):
                 @pl.when(z != s)
                 def _():
                     s3_copy(s).wait_recv()
-                    pick[y, s] = part3[1 + s]
-            pick[y, z] = part3[0]
+                    held[s] = part3[1 + s]
+            held[z] = part3[0]
+            pick[y, pl.ds(core * 4, 4)] = held[pl.ds(core * 4, 4)]
             for d in others:
                 s4_copy(d).start()
 
-        @pl.when(j == 4)
-        def _():
-            for d in others:
-                @pl.when((q + 8 - d) % 8 == z)
+    def s4_on():
+        for d in others:
+            @pl.when((q + 8 - d) % 8 == z)
+            def _():
+                s4_copy(d).wait_recv()
+        for d in others:
+            s5_copy(d).start()
+
+    def s5_on():
+        for d in others:
+            s5_copy(d).wait_recv()
+        s6_copy().start()
+
+    def y2_on():
+        for d in others:
+            y_copy(2, d).wait_recv()
+        k_copy(2).start()
+
+    def y3_on():
+        for d in others:
+            y_copy(3, d).wait_recv()
+        for d in range(1, 4):
+            x_copy(3, d).start()
+
+    def x3_on():
+        for d in range(1, 4):
+            x_copy(3, d).wait_recv()
+        k_copy(3).start()
+
+    plan = {
+        0: [lambda: k_copy(0).wait_recv()],
+        1: [y3_on],
+        2: [lambda: k_copy(1).wait_recv(), y2_on],
+        3: [s1_on],
+        4: [lambda: k_copy(2).wait_recv(), lambda: p_hop(1)],
+        5: [x3_on],
+        6: [s2_on],
+        8: [lambda: k_copy(3).wait_recv(), lambda: p_hop(2), s3_on],
+        11: [s4_on],
+        12: [lambda: p_hop(3)],
+        15: [s5_on],
+    }
+
+    def arrive(j, half):
+        for at, parts in plan.items():
+            if at % 2 == half:
+                @pl.when(j == at // 2)
                 def _():
-                    s4_copy(d).wait_recv()
-            for d in others:
-                s5_copy(d).start()
+                    for part in parts:
+                        part()
 
     def step(j, carry):
-        arrive(j)
+        arrive(j, 0)
         jm = jnp.maximum(j - 1, 0)
         jn = jnp.minimum(j + 1, NB - 1)
         now = pl.ds(pl.multiple_of(j * B, B), B)
@@ -328,10 +346,13 @@
             lu[was_below, part, last] = done
             upper = jnp.where(block > j, 0, 1)
             t = -dot(lu[upper, part, :], row_j)
-            source = piv[j, block * 4 + half * 2 : block * 4 + half * 2 + 2].reshape(64, B)
+            low = (block % 2) * 4 + half * 2
+            source = piv[j, block // 2, low : low + 2].reshape(64, B)
             on = jnp.where(block == j, 1.0, 0.0).astype(F32)
             t = t + jnp.where(block > j, source.astype(F32), 0.0) + eye[half * 64 : half * 64 + 64, :] * on
             tcol[part, :] = t.astype(BF16)
+            if p == 7:
+                arrive(j, 1)
             if p == 3:
                 row_next = lu[0, after, :]
                 quad[...] = dot(row_next, row_next)
@@ -347,15 +368,6 @@
         part = slice(i * 256, (i + 1) * 256)
         lu[1, part, N - B : N] = dot(tcol[part, :], w_ref[...]).astype(BF16)
 
-    for d in others:
-        s5_copy(d).wait_recv()
-    raw = jnp.concatenate(
-        [jnp.concatenate([pick[i, c] for i in range(8)], axis=0) for c in range(NB)], axis=1
-    )
-    for c in range(4):
-        cols = slice(c * 256, (c + 1) * 256)
-        deep = (c + 1) * 256
-        low_w[:, cols] = dot(raw[:, :deep], lu[1, :deep, cols], NN).astype(BF16)
     for way in range(2):
         p_copy(3, way).wait_recv()
     for i in range(8):
@@ -366,13 +378,26 @@
             deep = (c + 1) * 256
             fac[part, cols] = dot(mine[:, :deep], lu[1, :deep, cols], NN).astype(BF16)
         own_out[part, :] = fac[part, pl.ds(pl.multiple_of(z * B, B), B)]
+
+    s6_copy().wait_recv()
+    raw = jnp.concatenate(
+        [jnp.concatenate([pick[i, c] for i in range(8)], axis=0) for c in range(NB)], axis=1
+    )
+    for c in range(4):
+        cols = slice(c * 256, (c + 1) * 256)
+        deep = (c + 1) * 256
+        low_w[:, cols] = dot(raw[:, :deep], lu[1, :deep, cols], NN).astype(BF16)
+    for i in range(8):
+        part = slice(i * B, (i + 1) * B)
         update = dot(fac[part, :], low_w[...])
         left = slab[part, :].astype(F32) - update
         for c in range(2):
             cols = slice(c * B, (c + 1) * B)
             slab_out[part, cols] = (left[:, cols] * pattern[i, c].astype(F32)).astype(BF16)
 
-    for g in range(1, 3):
+    for g in range(4):
+        for d in others:
+            y_copy(g, d).wait_send()
         for d in range(1, 4):
             x_copy(g, d).wait_send()
         k_copy(g).wait_send()
@@ -380,9 +405,6 @@
         for way in range(2):
             p_copy(hop, way).wait_send()
     for d in others:
-        for g in range(2):
-            y_copy(g, d).wait_send()
-            q_copy(g, d).wait_send()
         c_copy(d).wait_send()
         s1_copy(d).wait_send()
         s2_copy(d).wait_send()
@@ -391,6 +413,8 @@
         @pl.when(z == q)
         def _():
             s4_copy(d).wait_send()
+
+    s6_copy().wait_send()
 
     @pl.when(z != q)
     def _():
@@ -410,12 +434,13 @@
         in_specs=[vmem, vmem, vmem, smem, smem],
         out_specs=[vmem, vmem],
         scratch_shapes=[
-            pltpu.VMEM((8, 32, 2, 16, B), BF16),
+            pltpu.VMEM((8, 4, 8, 2, 16, B), BF16),
             pltpu.VMEM((8, 8, B), I32),
             pltpu.VMEM((8, 2 * B, B), BF16),
             pltpu.VMEM((8, 2 * B, B), BF16),
             pltpu.VMEM((8, 2 * B, B), BF16),
             pltpu.VMEM((9, 32, B), BF16),
+            pltpu.VMEM((8, 32, B), BF16),
             pltpu.VMEM((8, 8, 32, B), BF16),
             pltpu.VMEM((8, N, B), BF16),
             pltpu.VMEM((2, N, N), BF16),
@@ -424,12 +449,11 @@
             pltpu.VMEM((B, B), BF16),
             pltpu.VMEM((2 * B, N), BF16),
             pltpu.VMEM((N, N), BF16),
-            dma((2, 8)), dma((2, 8)), dma((2, 8)), dma((2, 8)),
-            dma((3, 4)), dma((3, 4)), dma((3,)), dma((3,)),
+            dma((4, 8)), dma((4, 8)), dma((4, 4)), dma((4, 4)), dma((4,)), dma((4,)),
             dma((8,)), dma((8,)), dma((4, 2)), dma((4, 2)),
             dma((8,)), dma((8,)), dma((8,)), dma((8,)),
             dma, dma((8,)),
-            dma((8,)), dma((8,)), dma((8,)), dma((8,)),
+            dma((8,)), dma((8,)), dma((8,)), dma((8,)), dma, dma,
         ],
         compiler_params=pltpu.CompilerParams(
             collective_id=0, has_side_effects=True, vmem_limit_bytes=56 * 2**20

time: 80.5 us -> 71.1 us (0.88)
  the two profiles are of different devices: /device:TPU:5 before, /device:TPU:1 now
where the time goes in v3:
time: 71.1 us; the launch traced here: 69.7 us
  Pallas kernels  65.2 us (92%)
  local copies, waits for them, and re-layouts  3.87 us (5%)
    pallas_call x1, Pallas kernels, shards(): pl.pallas_call(kernel, out_shape=[jax.ShapeDtypeStruct((N, B), BF16), jax...  65.2 us
    unnamed x5, local copies, waits for them, and re-layouts  3.87 us

profile of v3, /device:TPU:1, one launch (start us, length us, event | category | flops | bytes accessed | tf_op | source)
XLA Modules:
  0.0 69.7 jit_solution(2635132035239397886)
XLA Ops:
  0.6 1.3 %copy.7.pattern = s32[8,2]{1,0:T(8,128)} copy(s32[8,2]{0,1:T(2,128)} %param.8) | data formatting | bytes 128 | tf_op args[3]
  2.0 65.2 %shard_map.68 = (bf16[1024,128]{1,0:T(8,128)(2,1)}, bf16[1024,256]{1,0:T(8,128)(2,1)}) custom-call(f32[16,1024]{1,0:T(8,128)} %pivot.1, bf16[1024,128]{1,0:T(8,128)(2,1)} %panel.1, bf16[1024,256]{1,0:T(8,128)(2,1)} %slab.1, s32[8,2]{1,0:T(8,128)} %copy.7.pattern, s32[2]{0:T(128)} %col_source.1), custom_call_target="tpu_custom_call" | custom-call | flops 5000000000 | bytes 2097152 | tf_op jit(solution)/shard_map/pallas_call | solution.py:428
  67.2 0.0 copy-start
  67.2 1.7 %copy.10 = bf16[1024,128]{1,0:T(8,128)(2,1)} copy(bf16[1024,128]{1,0:T(8,128)(2,1)} %get-tuple-element.4) | data formatting | bytes 524288
  68.9 0.0 copy-done
  68.9 0.8 %copy.11 = bf16[1024,256]{1,0:T(8,128)(2,1)} copy(bf16[1024,256]{1,0:T(8,128)(2,1)S(1)} %copy-done) | data formatting | bytes 1048576
Async XLA Ops:
  67.2 1.7 %copy-start = (bf16[1024,256]{1,0:T(8,128)(2,1)S(1)}, bf16[1024,256]{1,0:T(8,128)(2,1)}, u32[]{:S(2)}) copy-start(bf16[1024,256]{1,0:T(8,128)(2,1)} %get-tuple-element.5) | copy-start | bytes 1572868

commit v4 on v3

--- a/solution.py
+++ b/solution.py
@@ -11,6 +11,18 @@
 N = 1024
 MESH = pl.DeviceIdType.MESH
 GROUPS = (slice(0, 1), slice(1, 2), slice(2, 4), slice(4, 8))
+ASIDES = (
+    (0, ("finish", (0, 1, 2, 3))),
+    (1, ("finish", (4, 5, 6, 7))),
+    (4, ("begin", (0,))),
+    (5, ("begin", (1,))),
+    (6, ("begin", (2,))),
+    (7, ("begin", (3,))),
+    (9, ("begin", (4,))),
+    (10, ("begin", (5,))),
+    (11, ("begin", (6,))),
+    (12, ("begin", (7,))),
+)
 NT = (((1,), (1,)), ((), ()))
 NN = (((1,), (0,)), ((), ()))
 
@@ -68,11 +80,18 @@
             w_ref[8 * p - 8 : 8 * p + 8, :] = jnp.concatenate([before, w], 0).astype(BF16)
         full = full * inverse
         spread = [row_spread(full, k) for k in range(8)]
-        for q in range(p + 1, 16):
+        for q in range(p + 1, min(p + 3, 16)):
             v = rows[q]
             t = [lane_spread(v, 8 * p + k) * spread[k] for k in range(8)]
             total = ((t[0] + t[1]) + (t[2] + t[3])) + ((t[4] + t[5]) + (t[6] + t[7]))
             rows[q] = jnp.where(inside, 0.0, v) - total
+        if p < 13:
+            far = jnp.concatenate(rows[p + 3 :], 0) if p < 12 else rows[15]
+            zero = jnp.zeros((8, B), F32)
+            padded = jnp.concatenate([zero] * p + [full] + [zero] * (15 - p), 0).astype(BF16)
+            total = dot(far.astype(BF16), padded, NN)
+            for i, q in enumerate(range(p + 3, 16)):
+                rows[q] = jnp.where(inside, 0.0, rows[q]) - total[8 * i : 8 * i + 8]
         if more:
             cols = ahead
         aside(p)
@@ -80,9 +99,9 @@
 
 def kernel(
     pivot, panel, slab, pattern, col_source, own_out, slab_out,
-    piv, cs, marked, part1, part2, part3, held, pick, rows, lu, tcol, quad, w_ref, low_w, fac,
+    piv, cs, marked, part0, chip, part1, part2, part3, held, pick, rows, lu, tcol, quad, w_ref, low_w, fac,
     y_send, y_recv, x_send, x_recv, k_send, k_recv, c_send, c_recv, p_send, p_recv,
-    s1_send, s1_recv, s2_send, s2_recv, s3_send, s3_recv, s4_send, s4_recv, s5_send, s5_recv, s6_send, s6_recv,
+    s1_send, s1_recv, s2_send, s2_recv, s3_send, s3_recv, s4_send, s4_recv, s5_send, s5_recv, s6_send, s6_recv, s0_send, s0_recv,
 ):
     r = lax.axis_index("row")
     z = lax.axis_index("col")
@@ -144,9 +163,14 @@
         for way in range(2):
             p_copy(hop, way).start()
 
+    def s0_copy():
+        return remote(
+            marked.at[:, 1 - core], part0, s0_send, s0_recv, (r + 1 - 2 * core, z)
+        )
+
     def s1_copy(d):
         return remote(
-            marked.at[(q + d) % 8], part1.at[d], s1_send.at[d], s1_recv.at[d], at_q(d)
+            chip.at[(x + d) % 4], part1.at[d], s1_send.at[d], s1_recv.at[d], at_x(d)
         )
 
     def s2_copy(d):
@@ -197,16 +221,16 @@
     for g in (1, 3):
         for d in others:
             y_copy(g, d).start()
+    p_hop(0)
     rows[z] = panel[...]
     lu[...] = jnp.zeros_like(lu)
     quad[...] = jnp.zeros_like(quad)
     tcol[...] = jnp.zeros_like(tcol)
     w_ref[...] = jnp.zeros_like(w_ref)
-    for g in (0, 1):
-        for d in others:
-            y_copy(g, d).wait_recv()
-        for d in range(1, 4):
-            x_copy(g, d).start()
+    for d in others:
+        y_copy(0, d).wait_recv()
+    for d in range(1, 4):
+        x_copy(0, d).start()
 
     for d in others:
         c_copy(d).wait_recv()
@@ -218,30 +242,39 @@
             for s in range(8):
                 here = panel[s * B : (s + 1) * B, :].astype(F32)
                 total = jnp.where(wanted == r * 8 + s, here, total)
-            marked[pair, t * B : (t + 1) * B, :] = total.astype(BF16)
+            marked[pair // 2, pair % 2, t * B : (t + 1) * B, :] = total.astype(BF16)
         return carry
 
     lax.fori_loop(0, 8, mark, 0)
-    for d in others:
+    s0_copy().start()
+    for d in others:
+        y_copy(1, d).wait_recv()
+    for d in range(1, 4):
+        x_copy(1, d).start()
+    for d in range(1, 4):
+        x_copy(2, d).wait_recv()
+    for d in others:
+        y_copy(2, d).start()
+    for d in range(1, 4):
+        x_copy(0, d).wait_recv()
+    k_copy(0).start()
+    s0_copy().wait_recv()
+    for i in range(4):
+        chip[i] = marked[i, core] + part0[i]
+    for d in range(1, 4):
         s1_copy(d).start()
     for d in range(1, 4):
-        x_copy(2, d).wait_recv()
-    for d in others:
-        y_copy(2, d).start()
-    p_hop(0)
-    for g in (0, 1):
-        for d in range(1, 4):
-            x_copy(g, d).wait_recv()
-        k_copy(g).start()
+        x_copy(1, d).wait_recv()
+    k_copy(1).start()
 
     def block_rows(column, block):
         return piv[column, block // 2, pl.ds((block % 2) * 4, 4)].reshape(B, B)
 
     def s1_on():
-        total = marked[q].astype(F32)
-        for d in others:
+        total = chip[x].astype(F32)
+        for d in range(1, 4):
             s1_copy(d).wait_recv()
-        for d in others:
+        for d in range(1, 4):
             total += part1[d].astype(F32)
         part2[0] = total.astype(BF16)
         for d in others:
@@ -303,22 +336,23 @@
 
     plan = {
         0: [lambda: k_copy(0).wait_recv()],
-        1: [y3_on],
-        2: [lambda: k_copy(1).wait_recv(), y2_on],
-        3: [s1_on],
-        4: [lambda: k_copy(2).wait_recv(), lambda: p_hop(1)],
-        5: [x3_on],
-        6: [s2_on],
-        8: [lambda: k_copy(3).wait_recv(), lambda: p_hop(2), s3_on],
-        11: [s4_on],
-        12: [lambda: p_hop(3)],
-        15: [s5_on],
+        1: [lambda: p_hop(1)],
+        2: [y3_on],
+        4: [lambda: k_copy(1).wait_recv()],
+        5: [y2_on],
+        6: [s1_on],
+        8: [lambda: k_copy(2).wait_recv()],
+        12: [s2_on],
+        13: [x3_on, lambda: p_hop(2)],
+        16: [lambda: k_copy(3).wait_recv(), s3_on],
+        22: [s4_on],
+        24: [lambda: p_hop(3)],
     }
 
-    def arrive(j, half):
+    def arrive(j, quarter):
         for at, parts in plan.items():
-            if at % 2 == half:
-                @pl.when(j == at // 2)
+            if at % 4 == quarter:
+                @pl.when(j == at // 4)
                 def _():
                     for part in parts:
                         part()
@@ -338,24 +372,33 @@
             lax.broadcasted_iota(I32, (B, B), 0) == lax.broadcasted_iota(I32, (B, B), 1), 1.0, 0.0
         ).astype(F32)
 
+        def finish(blocks):
+            done = dot(tcol[blocks[0] * B : (blocks[-1] + 1) * B, :], w_old).astype(BF16)
+            for i, block in enumerate(blocks):
+                was_below = jnp.where(block > jm, 0, 1)
+                lu[was_below, block * B : (block + 1) * B, last] = done[i * B : (i + 1) * B]
+
+        def begin(blocks):
+            known = jnp.concatenate(
+                [lu[jnp.where(b > j, 0, 1), b * B : (b + 1) * B, :] for b in blocks], axis=0
+            )
+            t = dot(known, row_j)
+            for i, block in enumerate(blocks):
+                start = jnp.where(block > j, block_rows(j, block).astype(F32), 0.0)
+                start = jnp.where(block == j, eye, start)
+                tcol[block * B : (block + 1) * B, :] = (
+                    start - t[i * B : (i + 1) * B]
+                ).astype(BF16)
+
         def aside(p):
-            block, half = p // 2, p % 2
-            part = slice(p * 64, (p + 1) * 64)
-            was_below = jnp.where(block > jm, 0, 1)
-            done = dot(tcol[part, :], w_old).astype(BF16)
-            lu[was_below, part, last] = done
-            upper = jnp.where(block > j, 0, 1)
-            t = -dot(lu[upper, part, :], row_j)
-            low = (block % 2) * 4 + half * 2
-            source = piv[j, block // 2, low : low + 2].reshape(64, B)
-            on = jnp.where(block == j, 1.0, 0.0).astype(F32)
-            t = t + jnp.where(block > j, source.astype(F32), 0.0) + eye[half * 64 : half * 64 + 64, :] * on
-            tcol[part, :] = t.astype(BF16)
-            if p == 7:
-                arrive(j, 1)
+            if p in (3, 7, 11):
+                arrive(j, (p + 1) // 4)
             if p == 3:
                 row_next = lu[0, after, :]
                 quad[...] = dot(row_next, row_next)
+            for at, (do, blocks) in ASIDES:
+                if at == p:
+                    (finish if do == "finish" else begin)(blocks)
 
         factor([diagonal[8 * i : 8 * i + 8, :] for i in range(16)], w_ref, aside)
         new = dot(tcol[after, :], w_ref[...]).astype(BF16)
@@ -371,6 +414,8 @@
     for way in range(2):
         p_copy(3, way).wait_recv()
     for i in range(8):
+        if i == 2:
+            s5_on()
         part = slice(i * B, (i + 1) * B)
         mine = jnp.concatenate([rows[c, part, :] for c in range(NB)], axis=1)
         for c in range(4):
@@ -393,7 +438,7 @@
         left = slab[part, :].astype(F32) - update
         for c in range(2):
             cols = slice(c * B, (c + 1) * B)
-            slab_out[part, cols] = (left[:, cols] * pattern[i, c].astype(F32)).astype(BF16)
+            slab_out[part, cols] = (left[:, cols] * pattern[c, i].astype(F32)).astype(BF16)
 
     for g in range(4):
         for d in others:
@@ -404,9 +449,11 @@
     for hop in range(4):
         for way in range(2):
             p_copy(hop, way).wait_send()
+    s0_copy().wait_send()
+    for d in range(1, 4):
+        s1_copy(d).wait_send()
     for d in others:
         c_copy(d).wait_send()
-        s1_copy(d).wait_send()
         s2_copy(d).wait_send()
         s5_copy(d).wait_send()
 
@@ -436,8 +483,10 @@
         scratch_shapes=[
             pltpu.VMEM((8, 4, 8, 2, 16, B), BF16),
             pltpu.VMEM((8, 8, B), I32),
-            pltpu.VMEM((8, 2 * B, B), BF16),
-            pltpu.VMEM((8, 2 * B, B), BF16),
+            pltpu.VMEM((4, 2, 2 * B, B), BF16),
+            pltpu.VMEM((4, 2 * B, B), BF16),
+            pltpu.VMEM((4, 2 * B, B), BF16),
+            pltpu.VMEM((4, 2 * B, B), BF16),
             pltpu.VMEM((8, 2 * B, B), BF16),
             pltpu.VMEM((9, 32, B), BF16),
             pltpu.VMEM((8, 32, B), BF16),
@@ -453,7 +502,7 @@
             dma((8,)), dma((8,)), dma((4, 2)), dma((4, 2)),
             dma((8,)), dma((8,)), dma((8,)), dma((8,)),
             dma, dma((8,)),
-            dma((8,)), dma((8,)), dma((8,)), dma((8,)), dma, dma,
+            dma((8,)), dma((8,)), dma((8,)), dma((8,)), dma, dma, dma, dma,
         ],
         compiler_params=pltpu.CompilerParams(
             collective_id=0, has_side_effects=True, vmem_limit_bytes=56 * 2**20
@@ -461,7 +510,7 @@
         cost_estimate=pl.CostEstimate(
             flops=5 * 10**9, bytes_accessed=2 * 2**20, transcendentals=0
         ),
-    )(pivot, panel, slab, pattern, col_source)
+    )(pivot, panel, slab, pattern.T, col_source)
 
 
 def solution(mesh):

time: 71.1 us -> 64 us (0.900); the launches traced: 69.7 us -> 63.9 us
  Pallas kernels: 65.2 us -> 60.7 us
  local copies, waits for them, and re-layouts: 3.87 us -> 2.52 us
    pallas_call x1, Pallas kernels: 65.2 us -> 60.7 us  [shards(): pl.pallas_call(kernel, out_shape=[jax.ShapeDtypeStruct((N, B), BF16), jax...]
    unnamed x5 -> x4, local copies, waits for them, and re-layouts: 3.87 us -> 2.52 us
where the time goes in v4:
time: 64 us; the launch traced here: 63.9 us
  Pallas kernels  60.7 us (95%)
  local copies, waits for them, and re-layouts  2.52 us (4%)
  between operations  0.65 us (1%)
    pallas_call x1, Pallas kernels, shards(): pl.pallas_call(kernel, out_shape=[jax.ShapeDtypeStruct((N, B), BF16), jax...  60.7 us
    unnamed x4, local copies, waits for them, and re-layouts  2.52 us

profile of v4, /device:TPU:1, one launch (start us, length us, event | category | flops | bytes accessed | tf_op | source)
XLA Modules:
  0.0 63.9 jit_solution(1341597327368372271)
XLA Ops:
  0.6 60.7 %shard_map.68 = (bf16[1024,128]{1,0:T(8,128)(2,1)}, bf16[1024,256]{1,0:T(8,128)(2,1)}) custom-call(f32[16,1024]{1,0:T(8,128)} %pivot.1, bf16[1024,128]{1,0:T(8,128)(2,1)} %panel.1, bf16[1024,256]{1,0:T(8,128)(2,1)} %slab.1, s32[2,8]{1,0:T(2,128)} %bitcast.1, s32[2]{0:T(128)} %col_source.1), custom_call_target="tpu_custom_call" | custom-call | flops 5000000000 | bytes 2097152 | tf_op jit(solution)/shard_map/pallas_call | solution.py:475
  61.3 0.0 copy-start
  61.3 1.7 %copy.9 = bf16[1024,128]{1,0:T(8,128)(2,1)} copy(bf16[1024,128]{1,0:T(8,128)(2,1)} %get-tuple-element.4) | data formatting | bytes 524288
  63.1 0.0 copy-done
  63.1 0.8 %copy.10 = bf16[1024,256]{1,0:T(8,128)(2,1)} copy(bf16[1024,256]{1,0:T(8,128)(2,1)S(1)} %copy-done) | data formatting | bytes 1048576
Async XLA Ops:
  61.3 1.7 %copy-start = (bf16[1024,256]{1,0:T(8,128)(2,1)S(1)}, bf16[1024,256]{1,0:T(8,128)(2,1)}, u32[]{:S(2)}) copy-start(bf16[1024,256]{1,0:T(8,128)(2,1)} %get-tuple-element.5) | copy-start | bytes 1572868

commit v5 on v4

--- a/solution.py
+++ b/solution.py
@@ -413,15 +413,15 @@
 
     for way in range(2):
         p_copy(3, way).wait_recv()
-    for i in range(8):
-        if i == 2:
+    for i in range(4):
+        if i == 1:
             s5_on()
-        part = slice(i * B, (i + 1) * B)
-        mine = jnp.concatenate([rows[c, part, :] for c in range(NB)], axis=1)
+        part = slice(i * 256, (i + 1) * 256)
         for c in range(4):
             cols = slice(c * 256, (c + 1) * 256)
-            deep = (c + 1) * 256
-            fac[part, cols] = dot(mine[:, :deep], lu[1, :deep, cols], NN).astype(BF16)
+            deep = 2 * (c + 1)
+            mine = jnp.concatenate([rows[k, part, :] for k in range(deep)], axis=1)
+            fac[part, cols] = dot(mine, lu[1, : deep * B, cols], NN).astype(BF16)
         own_out[part, :] = fac[part, pl.ds(pl.multiple_of(z * B, B), B)]
 
     s6_copy().wait_recv()
@@ -432,13 +432,15 @@
         cols = slice(c * 256, (c + 1) * 256)
         deep = (c + 1) * 256
         low_w[:, cols] = dot(raw[:, :deep], lu[1, :deep, cols], NN).astype(BF16)
-    for i in range(8):
-        part = slice(i * B, (i + 1) * B)
+    for i in range(2):
+        part = slice(i * 512, (i + 1) * 512)
         update = dot(fac[part, :], low_w[...])
-        left = slab[part, :].astype(F32) - update
-        for c in range(2):
-            cols = slice(c * B, (c + 1) * B)
-            slab_out[part, cols] = (left[:, cols] * pattern[c, i].astype(F32)).astype(BF16)
+        for k in range(4):
+            for c in range(2):
+                cols = slice(c * B, (c + 1) * B)
+                here = slice(i * 512 + k * B, i * 512 + (k + 1) * B)
+                left = slab[here, cols].astype(F32) - update[k * B : (k + 1) * B, cols]
+                slab_out[here, cols] = (left * pattern[c, i * 4 + k].astype(F32)).astype(BF16)
 
     for g in range(4):
         for d in others:

time: 64 us -> 63.4 us (level)
  no operation moved by 1% of the time
where the time goes in v5:
time: 63.4 us; the launch traced here: 63.3 us
  Pallas kernels  60.1 us (95%)
  local copies, waits for them, and re-layouts  2.52 us (4%)
  between operations  0.65 us (1%)
    pallas_call x1, Pallas kernels, shards(): pl.pallas_call(kernel, out_shape=[jax.ShapeDtypeStruct((N, B), BF16), jax...  60.1 us
    unnamed x4, local copies, waits for them, and re-layouts  2.52 us

profile of v5, /device:TPU:1, one launch (start us, length us, event | category | flops | bytes accessed | tf_op | source)
XLA Modules:
  0.0 63.3 jit_solution(8841459271843542045)
XLA Ops:
  0.6 60.1 %shard_map.68 = (bf16[1024,128]{1,0:T(8,128)(2,1)}, bf16[1024,256]{1,0:T(8,128)(2,1)}) custom-call(f32[16,1024]{1,0:T(8,128)} %pivot.1, bf16[1024,128]{1,0:T(8,128)(2,1)} %panel.1, bf16[1024,256]{1,0:T(8,128)(2,1)} %slab.1, s32[2,8]{1,0:T(2,128)} %bitcast.1, s32[2]{0:T(128)} %col_source.1), custom_call_target="tpu_custom_call" | custom-call | flops 5000000000 | bytes 2097152 | tf_op jit(solution)/shard_map/pallas_call | solution.py:477
  60.7 0.0 copy-start
  60.7 1.7 %copy.9 = bf16[1024,128]{1,0:T(8,128)(2,1)} copy(bf16[1024,128]{1,0:T(8,128)(2,1)} %get-tuple-element.4) | data formatting | bytes 524288
  62.5 0.0 copy-done
  62.5 0.8 %copy.10 = bf16[1024,256]{1,0:T(8,128)(2,1)} copy(bf16[1024,256]{1,0:T(8,128)(2,1)S(1)} %copy-done) | data formatting | bytes 1048576
Async XLA Ops:
  60.7 1.7 %copy-start = (bf16[1024,256]{1,0:T(8,128)(2,1)S(1)}, bf16[1024,256]{1,0:T(8,128)(2,1)}, u32[]{:S(2)}) copy-start(bf16[1024,256]{1,0:T(8,128)(2,1)} %get-tuple-element.5) | copy-start | bytes 1572868

commit v6 on v5

--- a/solution.py
+++ b/solution.py
@@ -337,15 +337,16 @@
     plan = {
         0: [lambda: k_copy(0).wait_recv()],
         1: [lambda: p_hop(1)],
-        2: [y3_on],
+        3: [y3_on],
         4: [lambda: k_copy(1).wait_recv()],
-        5: [y2_on],
-        6: [s1_on],
+        6: [y2_on],
+        7: [s1_on],
         8: [lambda: k_copy(2).wait_recv()],
-        12: [s2_on],
-        13: [x3_on, lambda: p_hop(2)],
-        16: [lambda: k_copy(3).wait_recv(), s3_on],
-        22: [s4_on],
+        13: [s2_on],
+        14: [x3_on, lambda: p_hop(2)],
+        16: [lambda: k_copy(3).wait_recv()],
+        17: [s3_on],
+        23: [s4_on],
         24: [lambda: p_hop(3)],
     }
 
@@ -414,7 +415,7 @@
     for way in range(2):
         p_copy(3, way).wait_recv()
     for i in range(4):
-        if i == 1:
+        if i == 2:
             s5_on()
         part = slice(i * 256, (i + 1) * 256)
         for c in range(4):

time: 63.4 us -> 64.2 us (1.013)
  Pallas kernels: 60.1 us -> 60.9 us
    pallas_call x1, Pallas kernels: 60.1 us -> 60.9 us  [shards(): pl.pallas_call(kernel, out_shape=[jax.ShapeDtypeStruct((N, B), BF16), jax...]
where the time goes in v6:
time: 64.2 us; the launch traced here: 64.1 us
  Pallas kernels  60.9 us (95%)
  local copies, waits for them, and re-layouts  2.52 us (4%)
  between operations  0.65 us (1%)
    pallas_call x1, Pallas kernels, shards(): pl.pallas_call(kernel, out_shape=[jax.ShapeDtypeStruct((N, B), BF16), jax...  60.9 us
    unnamed x4, local copies, waits for them, and re-layouts  2.52 us

profile of v6, /device:TPU:1, one launch (start us, length us, event | category | flops | bytes accessed | tf_op | source)
XLA Modules:
  0.0 64.1 jit_solution(6011436869587850850)
XLA Ops:
  0.6 60.9 %shard_map.68 = (bf16[1024,128]{1,0:T(8,128)(2,1)}, bf16[1024,256]{1,0:T(8,128)(2,1)}) custom-call(f32[16,1024]{1,0:T(8,128)} %pivot.1, bf16[1024,128]{1,0:T(8,128)(2,1)} %panel.1, bf16[1024,256]{1,0:T(8,128)(2,1)} %slab.1, s32[2,8]{1,0:T(2,128)} %bitcast.1, s32[2]{0:T(128)} %col_source.1), custom_call_target="tpu_custom_call" | custom-call | flops 5000000000 | bytes 2097152 | tf_op jit(solution)/shard_map/pallas_call | solution.py:478
  61.5 0.0 copy-start
  61.5 1.7 %copy.9 = bf16[1024,128]{1,0:T(8,128)(2,1)} copy(bf16[1024,128]{1,0:T(8,128)(2,1)} %get-tuple-element.4) | data formatting | bytes 524288
  63.3 0.0 copy-done
  63.3 0.8 %copy.10 = bf16[1024,256]{1,0:T(8,128)(2,1)} copy(bf16[1024,256]{1,0:T(8,128)(2,1)S(1)} %copy-done) | data formatting | bytes 1048576
Async XLA Ops:
  61.5 1.7 %copy-start = (bf16[1024,256]{1,0:T(8,128)(2,1)S(1)}, bf16[1024,256]{1,0:T(8,128)(2,1)}, u32[]{:S(2)}) copy-start(bf16[1024,256]{1,0:T(8,128)(2,1)} %get-tuple-element.5) | copy-start | bytes 1572868
